TPU v7x, 32 devices: a whole 2x2x4 slice. The times are simulated.
32 devices in a mesh: groups: 2 (over x), mp: 16 (over z, y, core).
Axes of the slice: x: 2, y: 2, z: 4, core: 2. Of those that a mesh axis runs over, the one named last changes fastest.
Arguments:
- tokens_in: bfloat16 [1024, 6144], P('groups', 'mp'), parts along dimension 0
- attn_gain: float32 [12288], P(('groups', 'mp')), parts along dimension 0, may hold values from 0.1 to 1.9
- w_latent: bfloat16 [12288, 512], P(('groups', 'mp')), parts along dimension 0, may hold values from -0.078125 to 0.078125
- w_query: bfloat16 [12288, 512], P(('groups', 'mp')), parts along dimension 0
- w_key_up: bfloat16 [1024, 512], P('groups', 'mp'), parts along dimension 0, may hold values from -0.25 to 0.25
- w_value_up: bfloat16 [1024, 512], P('groups', 'mp'), parts along dimension 0, may hold values from -0.25 to 0.25
- w_output: bfloat16 [1024, 6144], P('groups', 'mp'), parts along dimension 0, may hold values from -0.25 to 0.25
- ffn_gain: float32 [12288], P('groups'), parts along dimension 0, may hold values from 0.1 to 1.9
- routes: int32 [1024, 2], P('groups'), parts along dimension 0, may hold values from 0 to 3, as said below
- slots: int32 [1024, 2], P('groups'), parts along dimension 0, may hold values from 0 to 447, as said below
- gates: float32 [1024, 2], P('groups'), parts along dimension 0, may hold values from 0.2 to 1
- w_gate: bfloat16 [12288, 32768], P('groups', 'mp'), parts along dimension 0, may hold values from -0.078125 to 0.078125
- w_up: bfloat16 [12288, 32768], P('groups', 'mp'), parts along dimension 0, may hold values from -0.078125 to 0.078125
- w_down: bfloat16 [65536, 6144], P(('groups', 'mp')), parts along dimension 0, may hold values from -0.0625 to 0.0625
Outputs:
- attended: bfloat16 [1024, 6144], P('groups', 'mp'), parts along dimension 0
- expert_mix: bfloat16 [1024, 6144], P('groups', 'mp'), parts along dimension 0
There are 2 independent parts, one for each index of `groups`. A program takes and returns all parts, laid end to end along the dimension named above; each array names one. Nothing has to cross between parts.
Inputs may be any that keep to these rules, and one draw needn't show every extreme that they name: `routes`: each token names two different experts. No expert is named by more than 448 tokens, and one expert is named by exactly 448 tokens. slots[t,k] is the slot of token t in expert routes[t,k]; the tokens that name one expert have distinct slots, from 0 up to that expert's count minus one.
All inputs are finite; a program needn't handle non-finite values.
Results may differ from a plain program's by a relative error of at most 0.0085.
The roundings to bfloat16 on the way count: a program that leaves them out, or rounds other values in their place, can miss the bound.
Values may be sent and summed in bfloat16 or wider, within the bound.
No kernel may reach another device: no remote copies, remote signals or barrier semaphores. Data moves between devices by JAX's collectives and lax.ppermute only.
A program may use at most 192 MiB of HBM per device.

v0:
```python
import jax
import jax.numpy as jnp
from jax import lax
from jax.sharding import PartitionSpec as P

D = 6144
HD = 128
EXPERTS = 4
CAP = 448


epsilon = 1e-05


def from_partner(array, axis, bit):
    return lax.ppermute(array, axis, [(i, i ^ 1 << bit) for i in range(lax.axis_size(axis))])


def body(
    tokens_in,
    attn_gain,
    w_latent,
    w_query,
    w_key_up,
    w_value_up,
    w_output,
    ffn_gain,
    routes,
    slots,
    gates,
    w_gate,
    w_up,
    w_down,
):
    total_tokens = tokens_in.shape[0]
    local_cols = tokens_in.shape[1]
    devices = lax.axis_size("mp")
    my_index = lax.axis_index("mp")
    tokens_wide = tokens_in.astype(jnp.float32)
    normed = (tokens_wide * attn_gain).astype(jnp.bfloat16)
    square_part = jnp.sum(tokens_wide * tokens_wide, axis=1)
    latent_part = jnp.dot(normed, w_latent, preferred_element_type=jnp.float32)
    square_sum, latent_total = lax.psum((square_part, latent_part), "mp")
    scale_one = lax.rsqrt(square_sum / D + epsilon)
    latent = (scale_one[:, None] * latent_total).astype(jnp.bfloat16)
    head_count = w_query.shape[1] // HD
    query_terms = jnp.einsum(
        "tc,che->hte",
        normed,
        w_query.reshape(w_query.shape[0], head_count, HD),
        preferred_element_type=jnp.float32,
    )
    query_sum = lax.psum_scatter(
        query_terms.reshape(head_count * total_tokens, HD), "mp", scatter_dimension=0, tiled=True
    )
    block_rows = query_sum.shape[0]
    blocks = total_tokens // block_rows
    query_block = my_index % blocks
    row_scale = lax.dynamic_slice_in_dim(scale_one, query_block * block_rows, block_rows)
    query_rows = (row_scale[:, None] * query_sum).astype(jnp.bfloat16)
    key_map = w_key_up
    value_map = w_value_up
    quarter = w_key_up.shape[1]
    for bit_pos in range((HD // quarter).bit_length() - 1):
        other_key, other_value = from_partner((key_map, value_map), "mp", bit_pos)
        upper_half = my_index // 2**bit_pos % 2 == 1
        key_map = jnp.where(
            upper_half,
            jnp.concatenate([other_key, key_map], 1),
            jnp.concatenate([key_map, other_key], 1),
        )
        value_map = jnp.where(
            upper_half,
            jnp.concatenate([other_value, value_map], 1),
            jnp.concatenate([value_map, other_value], 1),
        )
    key_rows = jnp.dot(latent, key_map, preferred_element_type=jnp.float32).astype(jnp.bfloat16)
    value_rows = jnp.dot(latent, value_map, preferred_element_type=jnp.float32).astype(jnp.bfloat16)
    scores = jnp.dot(query_rows, key_rows.T, preferred_element_type=jnp.float32) * HD ** (-0.5)
    query_pos = query_block * block_rows + jnp.arange(block_rows, dtype=jnp.int32)
    key_pos = jnp.arange(total_tokens, dtype=jnp.int32)
    scores = jnp.where(key_pos[None, :] <= query_pos[:, None], scores, -jnp.inf)
    row_max = jnp.max(scores, axis=1, keepdims=True)
    exp_scores = jnp.exp(scores - row_max)
    softmax_rows = (exp_scores / jnp.sum(exp_scores, axis=1, keepdims=True)).astype(jnp.bfloat16)
    head_out = jnp.dot(softmax_rows, value_rows, preferred_element_type=jnp.float32).astype(
        jnp.bfloat16
    )
    output_map = w_output.reshape(head_count, HD, local_cols)
    shard_piece = lax.all_gather(head_out, "mp", axis=0, tiled=True)
    pair_count = shard_piece.shape[0] // block_rows
    stacked = shard_piece.reshape(pair_count, block_rows, HD)
    pair_ids = jnp.arange(pair_count, dtype=jnp.int32)
    chosen = jnp.take(output_map, pair_ids // blocks, axis=0)
    contrib = jnp.einsum("krh,khc->krc", stacked, chosen, preferred_element_type=jnp.float32)
    placing = ((pair_ids % blocks)[:, None] == jnp.arange(blocks, dtype=jnp.int32)[None, :]).astype(
        jnp.float32
    )
    placed = jnp.einsum("kb,krc->brc", placing, contrib, precision=lax.Precision.HIGHEST)
    attn_sum = placed.reshape(total_tokens, local_cols)
    attended = (tokens_wide + attn_sum).astype(jnp.bfloat16)
    shards = devices // EXPERTS
    slot_codes = slots * EXPERTS + routes
    code_range = jnp.arange(CAP * EXPERTS, dtype=jnp.int32)[:, None]
    selector = (
        (slot_codes[:, 0][None, :] == code_range) | (slot_codes[:, 1][None, :] == code_range)
    ).astype(jnp.bfloat16)
    buffer = jnp.dot(selector, attended, preferred_element_type=jnp.float32).astype(jnp.bfloat16)
    outgoing = jnp.broadcast_to(
        buffer.reshape(CAP, EXPERTS, 1, local_cols), (CAP, EXPERTS, shards, local_cols)
    ).reshape(CAP, devices * local_cols)
    expert_rows = lax.all_to_all(outgoing, "mp", split_axis=1, concat_axis=1, tiled=True)
    rows_wide = expert_rows.astype(jnp.float32)
    scale_two = lax.rsqrt(jnp.sum(rows_wide * rows_wide, axis=1) / D + epsilon)
    ffn_in = (rows_wide * scale_two[:, None] * ffn_gain).astype(jnp.bfloat16)
    gate_proj = jnp.dot(ffn_in, w_gate, preferred_element_type=jnp.float32)
    up_proj = jnp.dot(ffn_in, w_up, preferred_element_type=jnp.float32)
    activated = (jax.nn.silu(gate_proj) * up_proj).astype(jnp.bfloat16)
    partial_value = jnp.dot(activated, w_down, preferred_element_type=jnp.float32)
    incoming = lax.all_to_all(
        partial_value.reshape(CAP, devices, local_cols),
        "mp",
        split_axis=1,
        concat_axis=1,
        tiled=True,
    )
    summed = jnp.sum(incoming.reshape(CAP, EXPERTS, shards, local_cols), axis=2).reshape(
        CAP * EXPERTS, local_cols
    )
    code_row = jnp.arange(CAP * EXPERTS, dtype=jnp.int32)[None, :]
    weighting = gates[:, 0:1] * (slot_codes[:, 0:1] == code_row).astype(jnp.float32)
    weighting = weighting + gates[:, 1:2] * (slot_codes[:, 1:2] == code_row).astype(jnp.float32)
    mixed_cols = jnp.dot(weighting, summed, precision=lax.Precision.HIGHEST)
    return (attended, mixed_cols.astype(jnp.bfloat16))


def solution(mesh):
    placed = (
        P("groups", "mp"),
        P(("groups", "mp")),
        P(("groups", "mp"), None),
        P(("groups", "mp"), None),
        P("groups", "mp"),
        P("groups", "mp"),
        P("groups", "mp"),
        P("groups"),
        P("groups", None),
        P("groups", None),
        P("groups", None),
        P("groups", "mp"),
        P("groups", "mp"),
        P(("groups", "mp"), None),
    )
    return jax.shard_map(
        body,
        mesh=mesh,
        in_specs=placed,
        out_specs=(P("groups", "mp"), P("groups", "mp")),
        check_vma=False,
    )
```

profile of v0, /device:TPU:13, one launch (start us, length us, event | category | flops | bytes accessed | tf_op | source)
XLA Modules:
  0.0 660.8 jit_solution(10824370750922358369)
XLA Ops:
  7.3 2.6 fusion.39
  10.0 0.7 collective-permute-start
  10.8 2.6 fusion.35
  13.6 21.9 %psum.14 = f32[512]{0:T(512)S(1)} all-reduce(f32[512]{0:T(512)S(1)} %fusion.31), channel_id=1, replica_groups=mesh['groups'=2,'mp'=16] {'mp'}, use_global_device_ids=true, to_apply=%region_1.0 | all-reduce | flops 512 | bytes 4096 | tf_op jit(solution)/shard_map/psum | solution.py:43
  35.7 0.9 gather_fusion
  36.7 0.5 collective-permute-start.1
  37.2 1.0 collective-permute-start.3
  38.3 1.6 collective-permute-done.1
  39.9 64.1 %all-reduce.2.cloned.1.call-done = f32[512,512]{1,0:T(8,128)} async-done(((f32[512,512]{1,0:T(8,128)}), f32[512,512]{1,0:T(8,128)}) %all-reduce.2.cloned.1.call-update) | async-done | bytes 1048592 | tf_op jit(solution)/shard_map/psum | solution.py:43
  104.0 60.3 %reduce-scatter.2.cloned.1.call-done = f32[128,128]{1,0:T(8,128)} async-done(((f32[2048,128]{1,0:T(8,128)}), f32[128,128]{1,0:T(8,128)}) %reduce-scatter.2.cloned.1.call-update) | async-done | bytes 65552 | tf_op jit(solution)/shard_map/reduce_scatter | solution.py:53
  164.3 1.9 fusion.84
  166.4 1.7 fusion.30
  168.1 18.9 %all_gather.3 = bf16[2048,128]{1,0:T(8,128)(2,1)S(1)} all-gather(bf16[128,128]{1,0:T(8,128)(2,1)S(1)} %fusion.30), channel_id=1, replica_groups=mesh['groups'=2,'mp'=16] {'mp'}, dimensions={0}, use_global_device_ids=true | all-gather | bytes 557056 | tf_op jit(solution)/shard_map/all_gather | solution.py:90
  187.0 0.6 fusion.22
  187.7 2.9 fusion.8
  190.8 1.2 fusion.11
  191.9 0.4 broadcast_in_dim.21
  192.5 0.7 broadcast_in_dim.22
  193.2 127.6 %all_to_all.14 = bf16[448,16,384]{2,0,1:T(8,128)(2,1)S(1)} all-to-all(bf16[448,16,384]{2,0,1:T(8,128)(2,1)S(1)} %bitcast.50), channel_id=1, replica_groups=mesh['groups'=2,'mp'=16] {'mp'}, dimensions={1} | all-to-all | bytes 11010048 | tf_op jit(solution)/shard_map/all_to_all | solution.py:112
  320.8 1.2 fusion
  322.0 1.1 convert_bitcast_fusion
  323.1 5.6 copy.45
  328.8 20.8 %fusion.81 = f32[448,2048]{1,0:T(8,128)} fusion(bf16[6144,2048]{1,0:T(8,128)(2,1)} %param.25, f32[448,6144]{1,0:T(8,128)} %bitcast.51, f32[6144]{0:T(1024)S(1)} %copy-done.9, f32[448]{0:T(512)S(1)} %add_rsqrt_fusion), kind=kOutput, calls=%fused_computation.103 | convolution fusion | flops 11282546688 | bytes 39872256 | tf_op jit(solution)/shard_map/dot_general | solution.py:116
  349.5 21.2 %multiply_convert_fusion.1.clone.4 = bf16[448,2048]{1,0:T(8,128)(2,1)} fusion(f32[448,2048]{1,0:T(8,128)} %fusion.81, bf16[6144,2048]{1,0:T(8,128)(2,1)} %param.26, f32[448,6144]{1,0:T(8,128)} %bitcast.52, f32[6144]{0:T(1024)S(1)} %copy-done.9, f32[448]{0:T(512)S(1)} %add_rsqrt_fusion), kind=kOutput, calls=%fused_computation.7.clone.clone.clone.1 | convolution fusion | flops 11288051712 | bytes 41707264 | tf_op jit(solution)/shard_map/dot_general | solution.py:117
  370.7 15.4 %fusion.10 = f32[448,6144]{1,0:T(8,128)S(1)} fusion(bf16[2048,6144]{1,0:T(8,128)(2,1)} %param.27, bf16[448,2048]{1,0:T(8,128)(2,1)} %multiply_convert_fusion.1.clone.4), kind=kOutput, calls=%fused_computation.20 | convolution fusion | flops 11274289152 | bytes 38010880 | tf_op jit(solution)/shard_map/dot_general | solution.py:119
  386.1 5.1 copy.53
  391.3 5.9 all-to-all-start.1
  397.2 238.5 %all-to-all-done.1 = f32[448,16,384]{2,0,1:T(8,128)} async-done(((f32[448,16,384]{2,0,1:T(8,128)}), f32[448,16,384]{2,0,1:T(8,128)}, u32[]{:S(2)}, u32[]{:S(2)}) %all-to-all-start.1) | async-done | bytes 11010080 | tf_op jit(solution)/shard_map/all_to_all | solution.py:120
  635.7 5.2 bitcast_reduce_fusion
  641.0 1.8 copy.42
  642.7 2.1 reshape.117
  644.8 9.2 %fusion.25 = bf16[512,384]{1,0:T(8,128)(2,1)} fusion(f32[1792,384]{1,0:T(8,128)} %reshape.117, f32[512]{0:T(512)S(1)} %bitcast.61, s32[512]{0:T(512)S(1)} %bitcast.59, f32[512]{0:T(512)S(1)} %bitcast.60, s32[512]{0:T(512)S(1)} %bitcast.57), kind=kOutput, calls=%fused_computation.33 | convolution fusion | flops 4232642560 | bytes 3153920 | tf_op jit(solution)/shard_map/dot_general | solution.py:133
  (46 shorter events, 1.1 us)
Async XLA Ops:
  7.2 28.6 %copy-start = (bf16[512,384]{1,0:T(8,128)(2,1)S(1)}, bf16[512,384]{1,0:T(8,128)(2,1)}, u32[]{:S(2)}) copy-start(bf16[512,384]{1,0:T(8,128)(2,1)} %param.20) | copy-start | bytes 1179652
  7.2 6.2 copy-start.2
  7.2 28.4 %copy-start.7 = (s32[512,2]{0,1:T(2,128)S(1)}, s32[512,2]{0,1:T(2,128)}, u32[]{:S(2)}) copy-start(s32[512,2]{0,1:T(2,128)} %param.23) | copy-start | bytes 12292
  7.2 28.4 %copy-start.6 = (s32[512,2]{0,1:T(2,128)S(1)}, s32[512,2]{0,1:T(2,128)}, u32[]{:S(2)}) copy-start(s32[512,2]{0,1:T(2,128)} %param.22) | copy-start | bytes 12292
  7.2 96.8 %all-reduce.2.cloned.1.call-start = ((), (), s32[]{:S(2)}) async-start(), calls=%async_computation.4 | async-start | bytes 2097152 | tf_op jit(solution)/shard_map/psum | solution.py:43
  9.9 26.7 %copy-start.4 = (bf16[512,32]{0,1:T(8,128)(2,1)S(1)}, bf16[512,32]{0,1:T(8,128)(2,1)}, u32[]{:S(2)}) copy-start(bf16[512,32]{0,1:T(8,128)(2,1)} %param.18) | copy-start | bytes 98308
  9.9 27.3 %copy-start.5 = (bf16[512,32]{0,1:T(8,128)(2,1)S(1)}, bf16[512,32]{0,1:T(8,128)(2,1)}, u32[]{:S(2)}) copy-start(bf16[512,32]{0,1:T(8,128)(2,1)} %param.19) | copy-start | bytes 98308
  9.9 154.4 %reduce-scatter.2.cloned.1.call-start = ((), (), s32[]{:S(2)}) async-start(), calls=%async_computation.3 | async-start | bytes 1114112 | tf_op jit(solution)/shard_map/reduce_scatter | solution.py:53
  10.0 26.6 %collective-permute-start = (bf16[512,32]{0,1:T(8,128)(2,1)}, bf16[512,32]{0,1:T(8,128)(2,1)S(1)}, u32[]{:S(2)}, u32[]{:S(2)}) collective-permute-start(bf16[512,32]{0,1:T(8,128)(2,1)} %param.18), channel_id=1, source_target_pairs={{0,1},{1,0},{2,3},{3,2},{4,5},{5,4},{6,7},{7,6},{8,9},{9,8},{10,11... | collective-permute-start | bytes 98312 | tf_op jit(solution)/shard_map/ppermute | solution.py:16
  10.7 26.5 %collective-permute-start.2 = (bf16[512,32]{0,1:T(8,128)(2,1)}, bf16[512,32]{0,1:T(8,128)(2,1)S(1)}, u32[]{:S(2)}, u32[]{:S(2)}) collective-permute-start(bf16[512,32]{0,1:T(8,128)(2,1)} %param.19), channel_id=1, source_target_pairs={{0,1},{1,0},{2,3},{3,2},{4,5},{5,4},{6,7},{7,6},{8,9},{9,8},{10,11... | collective-permute-start | bytes 98312 | tf_op jit(solution)/shard_map/ppermute | solution.py:16
  36.7 3.2 collective-permute-start.1
  37.2 129.1 %collective-permute-start.3 = (bf16[512,64]{0,1:T(8,128)(2,1)S(1)}, bf16[512,64]{0,1:T(8,128)(2,1)S(1)}, u32[]{:S(2)}, u32[]{:S(2)}) collective-permute-start(bf16[512,64]{0,1:T(8,128)(2,1)S(1)} %maximum_select_fusion.7), channel_id=1, source_target_pairs={{0,2},{1,3},{2,0},{3,1},{4,6},{5,7},{6,4},{7,5},{8,10},{9,11},{10,... | collective-permute-start | bytes 196616 | tf_op jit(solution)/shard_map/ppermute | solution.py:16
  190.8 1.5 copy-start.3
  323.1 5.6 copy-start.9
  391.3 5.9 copy-start.8
  391.3 244.5 %all-to-all-start.1 = ((f32[448,16,384]{2,0,1:T(8,128)}), f32[448,16,384]{2,0,1:T(8,128)}, u32[]{:S(2)}, u32[]{:S(2)}) async-start(f32[448,16,384]{2,0,1:T(8,128)} %bitcast.49), calls=%async_computation.2 | async-start | bytes 22020096 | tf_op jit(solution)/shard_map/all_to_all | solution.py:120
  644.8 9.2 %copy-start.1 = (bf16[512,384]{1,0:T(8,128)(2,1)S(1)}, bf16[512,384]{1,0:T(8,128)(2,1)}, u32[]{:S(2)}) copy-start(bf16[512,384]{1,0:T(8,128)(2,1)} %param.20) | copy-start | bytes 1179652
Sparse Core Ops, SparseCore 0:
  11.5 92.4 all-reduce.1
  107.6 56.6 reduce-scatter.1
where the time goes:
time: 661 us
  waiting for transfers between devices  365 us (55%)
  blocking collectives  168 us (25%)
  matrix products  80.1 us (12%)
  local copies, waits for them, and re-layouts  16.9 us (3%)
  between operations  14.4 us (2%)
  starting transfers between devices  8.4 us (1%)
  other arithmetic  8.02 us (1%)
    all_to_all x1, waiting for transfers between devices, body(): lax.all_to_all(partial_value.reshape(CAP, devices, local_cols), 'mp', spl...  239 us
    all_to_all x1, blocking collectives, body(): lax.all_to_all(outgoing, 'mp', split_axis=1, concat_axis=1, tiled=True)  128 us
    psum x1, waiting for transfers between devices, body(): square_sum, latent_total = lax.psum((square_part, latent_part), 'mp')  64.1 us
    reduce_scatter x1, waiting for transfers between devices, body(): lax.psum_scatter(query_terms.reshape(head_count * total_tokens, HD), 'mp'...  60.3 us
    psum x1, blocking collectives, body(): square_sum, latent_total = lax.psum((square_part, latent_part), 'mp')  21.9 us
    dot_general x1, matrix products, body(): up_proj = jnp.dot(ffn_in, w_up, preferred_element_type=jnp.float32)  21.2 us
    dot_general x1, matrix products, body(): gate_proj = jnp.dot(ffn_in, w_gate, preferred_element_type=jnp.float32)  20.8 us
    all_gather x1, blocking collectives, body(): shard_piece = lax.all_gather(head_out, 'mp', axis=0, tiled=True)  18.9 us
  transfers between devices with their start and end apart: 7, of which 4 were waited for; matrix products, arithmetic and copies ran while one was open for 1% of the time, Pallas kernels for 0%

commit v1 on v0

v1 whole, which is shorter than its diff:
```python
import functools

import jax
import jax.numpy as jnp
from jax import lax
from jax.experimental import pallas as pl
from jax.experimental.pallas import tpu as pltpu
from jax.sharding import PartitionSpec as P

D = 6144
HD = 128
EXPERTS = 4
CAP = 448
QUAD = 4
MIB = 2**20


epsilon = 1e-05
f32 = jnp.float32
bf16 = jnp.bfloat16


def across(array, bit):
    return lax.ppermute(array, "mp", [(i, i ^ 1 << bit) for i in range(lax.axis_size("mp"))])


def across_plane(array, mask):
    return lax.ppermute(array, "mp", [(i, i ^ mask) for i in range(lax.axis_size("mp"))])


def to_plane(array, step):
    n = lax.axis_size("mp")
    return lax.ppermute(array, "mp", [(i, (i + QUAD * step) % n) for i in range(n)])


def wide_dot(a, b):
    return jnp.dot(a, b, preferred_element_type=f32)


def columns_at(array, start, width):
    return lax.dynamic_slice_in_dim(array, start, width, 1)


def rows_at(array, start, height):
    return lax.dynamic_slice_in_dim(array, start, height, 0)


def rolled_rows(array, start):
    return rows_at(jnp.concatenate([array, array], 0), start, array.shape[0])


def stage(*arrays):
    return lax.optimization_barrier(arrays)


def plane_groups(planes):
    return [[QUAD * p + q for p in range(planes)] for q in range(QUAD)]


def from_planes(array, plane, planes):
    if planes == EXPERTS:
        return [array] + [to_plane(array, -step) for step in range(1, planes)]
    every = lax.all_gather(array, "mp", axis_index_groups=plane_groups(planes))
    every = jnp.take(every, (jnp.arange(planes, dtype=jnp.int32) + plane) % planes, axis=0)
    return [every[step] for step in range(planes)]


def select_kernel(where_ref, selector_ref, scale_ref, gain_ref, a_ref, b_ref, c_ref, d_ref, out_ref):
    tokens = jnp.concatenate([a_ref[...], b_ref[...], c_ref[...], d_ref[...]], axis=0)
    rows = wide_dot(selector_ref[...], tokens)
    out_ref[...] = (rows * scale_ref[...] * gain_ref[where_ref[0]]).astype(bf16)


def select_rows(where, selector, scale, gain, pieces):
    width = pieces[0].shape[1]
    vmem = pl.BlockSpec(memory_space=pltpu.VMEM)
    return pl.pallas_call(
        select_kernel,
        in_specs=[pl.BlockSpec(memory_space=pltpu.SMEM)] + [vmem] * 7,
        out_specs=vmem,
        out_shape=jax.ShapeDtypeStruct((CAP, width), bf16),
        compiler_params=pltpu.CompilerParams(vmem_limit_bytes=16 * MIB),
        cost_estimate=pl.CostEstimate(
            flops=2 * CAP * 512 * width, bytes_accessed=2 * (512 + CAP) * width, transcendentals=0
        ),
    )(where.reshape(1), selector, scale, gain.reshape(-1, 1, width), *pieces)


def hidden_kernel(first, last, where_ref, rows_ref, gate_ref, up_ref, *refs):
    gate = wide_dot(rows_ref[...], gate_ref[...])
    up = wide_dot(rows_ref[...], up_ref[...])
    tile = gate.shape[1]
    here = pl.ds(pl.multiple_of(pl.program_id(0) * tile, tile), tile)
    if not first:
        sums_ref, _, *refs = refs
        gate = gate + sums_ref[0, :, here]
        up = up + sums_ref[1, :, here]
    out_ref, mark_ref = refs
    if not last:
        out_ref[0, :, here] = gate
        out_ref[1, :, here] = up
        mark_ref[...] = jnp.zeros_like(mark_ref)
        return
    activated = gate / (1.0 + jnp.exp(-gate)) * up
    out_ref[...] = activated.astype(bf16)
    peak = jnp.max(jnp.abs(activated).reshape(CAP // 8, 8, -1), axis=0)
    peak = jnp.max(peak, axis=1, keepdims=True)

    @pl.when(pl.program_id(0) == 0)
    def _():
        mark_ref[...] = jnp.zeros_like(mark_ref)

    mark_ref[...] = jnp.maximum(mark_ref[...], peak)


def hidden_part(where, rows, w_gate, w_up, before, last):
    width = rows.shape[1]
    units = w_gate.shape[1]
    tile = min(512, units)
    first = not before
    vmem = pl.BlockSpec(memory_space=pltpu.VMEM)
    weights = pl.BlockSpec((width, tile), lambda j, s: (s[0], j))
    if last:
        out_spec = pl.BlockSpec((CAP, tile), lambda j, s: (0, j))
        out_shape = jax.ShapeDtypeStruct((CAP, units), bf16)
    else:
        out_spec, out_shape = vmem, jax.ShapeDtypeStruct((2, CAP, units), f32)
    return pl.pallas_call(
        functools.partial(hidden_kernel, first, last),
        grid_spec=pltpu.PrefetchScalarGridSpec(
            num_scalar_prefetch=1,
            grid=(units // tile,),
            in_specs=[pl.BlockSpec((CAP, width), lambda j, s: (0, 0)), weights, weights]
            + [vmem] * len(before),
            out_specs=[out_spec, pl.BlockSpec((8, 128), lambda j, s: (0, 0))],
        ),
        out_shape=[out_shape, jax.ShapeDtypeStruct((8, 128), f32)],
        input_output_aliases={} if first or last else {4: 0},
        compiler_params=pltpu.CompilerParams(vmem_limit_bytes=40 * MIB),
        cost_estimate=pl.CostEstimate(
            flops=4 * CAP * width * units,
            bytes_accessed=4 * width * units,
            transcendentals=CAP * units,
        ),
    )(where.reshape(1), rows, w_gate, w_up, *before)


def down_kernel(blocks, marked, where_ref, act_ref, w_ref, *refs):
    product = wide_dot(act_ref[...], w_ref[...])
    half = product.shape[1] // 2
    upper = where_ref[blocks] == 1
    if marked:
        peak_ref, *refs = refs
    for index in range(blocks):

        @pl.when(pl.program_id(0) == index)
        def _():
            send_ref, keep_ref = refs[2 * index], refs[2 * index + 1]
            send_ref[:CAP] = jnp.where(upper, product[:, :half], product[:, half:])
            if marked and index == 0:
                send_ref[CAP:] = jnp.full((8, half), jnp.max(peak_ref[...]))
            keep_ref[...] = jnp.where(upper, product[:, half:], product[:, :half])


def down_parts(blocks, core, activated, w_down, width, peak=None):
    units = activated.shape[1]
    part = jax.ShapeDtypeStruct((CAP, width), f32)
    marked_part = jax.ShapeDtypeStruct((CAP + 8, width), f32)
    count = len(blocks)
    marked = peak is not None
    shapes = [part] * (2 * count)
    if marked:
        shapes[0] = marked_part
    parts = pl.pallas_call(
        functools.partial(down_kernel, count, marked),
        grid_spec=pltpu.PrefetchScalarGridSpec(
            num_scalar_prefetch=1,
            grid=(count,),
            in_specs=[
                pl.BlockSpec((CAP, units), lambda j, s: (0, 0)),
                pl.BlockSpec((units, 2 * width), lambda j, s: (0, s[j])),
            ]
            + [pl.BlockSpec((8, 128), lambda j, s: (0, 0))] * marked,
            out_specs=[pl.BlockSpec(shape.shape, lambda j, s: (0, 0)) for shape in shapes],
        ),
        out_shape=shapes,
        compiler_params=pltpu.CompilerParams(vmem_limit_bytes=40 * MIB),
        cost_estimate=pl.CostEstimate(
            flops=4 * CAP * units * width * count,
            bytes_accessed=4 * units * width * count,
            transcendentals=0,
        ),
    )(jnp.stack([*blocks, core]), activated, w_down, *([peak] if marked else []))
    return [(parts[2 * index], parts[2 * index + 1]) for index in range(count)]


def body(
    tokens_in,
    attn_gain,
    w_latent,
    w_query,
    w_key_up,
    w_value_up,
    w_output,
    ffn_gain,
    routes,
    slots,
    gates,
    w_gate,
    w_up,
    w_down,
):
    total_tokens, local_cols = tokens_in.shape
    planes = lax.axis_size("mp") // QUAD
    head_count = w_query.shape[1] // HD
    assert head_count == planes and planes % EXPERTS == 0
    latent_cols = w_latent.shape[1] // planes
    block = total_tokens // QUAD
    me = lax.axis_index("mp")
    plane, quarter = me // QUAD, me % QUAD
    side, core = quarter // 2, quarter % 2
    mine = 2 * core + side

    exact = planes == EXPERTS
    groups = plane_groups(planes)
    in_order = jnp.arange(QUAD, dtype=jnp.int32) ^ quarter
    block_order = jnp.arange(QUAD, dtype=jnp.int32) ^ mine

    tokens_wide = tokens_in.astype(f32)
    normed = (tokens_wide * attn_gain).astype(bf16)

    squares = jnp.sum(tokens_wide * tokens_wide, axis=1).reshape(1, total_tokens)

    def with_row(array, row):
        return jnp.concatenate(
            [array, jnp.pad(row, ((0, 7), (0, array.shape[1] - row.shape[1])))], axis=0
        )

    def projected(start):
        half = rows_at(normed, start * 2 * block, 2 * block)
        return jnp.concatenate([wide_dot(half, w_latent), wide_dot(half, w_query)], axis=1)

    sent = with_row(projected(1 - core), columns_at(squares, (1 - core) * 2 * block, 2 * block))
    (sent, squares) = stage(sent, squares)
    came = across(sent, 0)
    half_sum = projected(core) + came[: 2 * block]
    squares = columns_at(squares, core * 2 * block, 2 * block) + came[2 * block, : 2 * block][None]
    away = with_row(
        rows_at(half_sum, (1 - side) * block, block), columns_at(squares, (1 - side) * block, block)
    )
    stay = rows_at(half_sum, side * block, block)
    squares = columns_at(squares, side * block, block)
    away, stay, squares, tokens_in, w_key_up, w_value_up, w_output = stage(
        away, stay, squares, tokens_in, w_key_up, w_value_up, w_output
    )
    came = across(away, 1)
    plane_sum = stay + came[:block]
    squares = squares + came[block, :block][None]
    key_value_map = jnp.concatenate([w_key_up.T, w_value_up.T], axis=0)
    map_here = rolled_rows(w_output, plane * HD)
    pieces = []
    for mask in range(QUAD):
        block_there = mine ^ (2 * (mask % 2) + mask // 2)
        pieces.append(rows_at(tokens_in, block_there * block, block))
    plane_sum, squares, map_here, key_value_map, *pieces = stage(
        plane_sum, squares, map_here, key_value_map, *pieces
    )

    def share_of(target):
        return jnp.concatenate(
            [
                columns_at(plane_sum, target * latent_cols, latent_cols),
                columns_at(plane_sum, planes * latent_cols + target * HD, HD),
            ],
            axis=1,
        )

    if exact:
        sums, square_sum = share_of(plane), squares
        for step in range(1, planes):
            came = to_plane(with_row(share_of((plane + step) % planes), squares), step)
            sums = sums + came[:block]
            square_sum = square_sum + came[block, :block][None]
    else:
        square_sum = lax.psum(squares, "mp", axis_index_groups=groups)
        shares = jnp.stack([share_of(p) for p in range(planes)])
        sums = lax.all_to_all(shares, "mp", 0, 0, axis_index_groups=groups, tiled=True)
        sums = jnp.sum(sums, axis=0)
    maps = [key_value_map] + [across_plane(key_value_map, mask) for mask in range(1, QUAD)]
    scale_one = lax.rsqrt(square_sum / D + epsilon).reshape(block, 1)
    latent = (scale_one * sums[:, :latent_cols]).astype(bf16)
    query_rows = (scale_one * sums[:, latent_cols:]).astype(bf16)
    latent, query_rows, map_here, *maps = stage(latent, query_rows, map_here, *maps)

    latent = jnp.concatenate(from_planes(latent, plane, planes), axis=1)
    map_side = across(map_here, 1)
    narrow = key_value_map.shape[0] // 2
    maps = jnp.take(jnp.stack(maps), in_order, axis=0).reshape(QUAD, 2, narrow, -1)
    maps = maps.transpose(1, 0, 2, 3).reshape(2 * HD, -1).T
    maps = rolled_rows(maps, plane * latent_cols)
    latent, maps, map_here, map_side = stage(latent, maps, map_here, map_side)
    key_value = wide_dot(latent, maps).astype(bf16)
    key_value = jnp.concatenate([key_value, across(key_value, 1)], axis=0)
    columns = [map_here, across(map_here, 0), map_side, across(map_side, 0)]
    key_value, *columns = stage(key_value, *columns)
    key_value = jnp.concatenate([key_value, across(key_value, 0)], axis=0)
    scores = wide_dot(query_rows, key_value[:, :HD].T) * HD ** (-0.5)
    inside = jnp.arange(block, dtype=jnp.int32)
    key_pos = (block_order[:, None] * block + inside[None, :]).reshape(1, total_tokens)
    query_pos = (mine * block + inside)[:, None]
    scores = jnp.where(key_pos <= query_pos, scores, -jnp.inf)
    row_max = jnp.max(scores, axis=1, keepdims=True)
    exp_scores = jnp.exp(scores - row_max)
    softmax_rows = (exp_scores / jnp.sum(exp_scores, axis=1, keepdims=True)).astype(bf16)
    head_out = wide_dot(softmax_rows, key_value[:, HD:]).astype(bf16)
    head_out, routes, slots, gates, tokens_in, *columns = stage(
        head_out, routes, slots, gates, tokens_in, *columns
    )

    heads = jnp.concatenate(from_planes(head_out, plane, planes), axis=1)
    expert = plane // (planes // EXPERTS)
    slot_ids = jnp.arange(CAP, dtype=jnp.int32)
    slot_here = jnp.where(routes == expert, slots, -1)
    slot_arrived = jnp.take(slot_here.reshape(QUAD, block, 2), block_order, axis=0).reshape(-1, 2)
    chosen = (slot_arrived[:, 0][None, :] == slot_ids[:, None]) | (
        slot_arrived[:, 1][None, :] == slot_ids[:, None]
    )
    selector = chosen.astype(bf16)
    slot_gate = sum(
        jnp.sum(
            jnp.where(slot_here[:, k][None, :] == slot_ids[:, None], gates[:, k][None, :], 0.0),
            axis=1,
            keepdims=True,
        )
        for k in range(2)
    )
    output_map = jnp.take(jnp.stack(columns), in_order, axis=0)
    output_map = output_map.transpose(1, 0, 2).reshape(-1, QUAD * local_cols)
    pieces = [pieces[0]] + [across_plane(pieces[mask], mask) for mask in range(1, QUAD)]
    tokens_here = jnp.take(jnp.stack(pieces), in_order, axis=0)
    tokens_here = tokens_here.transpose(1, 0, 2).reshape(block, QUAD * local_cols)
    heads, selector, slot_gate, output_map, tokens_here = stage(
        heads, selector, slot_gate, output_map, tokens_here
    )

    attended_here = (tokens_here.astype(f32) + wide_dot(heads, output_map)).astype(bf16)
    squares = jnp.sum(jnp.square(attended_here.astype(f32)), axis=1).reshape(1, block)
    outgoing = [None] * QUAD

    def own_columns():
        for mask in range(QUAD):
            piece = columns_at(attended_here, (quarter ^ mask) * local_cols, local_cols)
            piece = piece if mask == 0 else across_plane(piece, mask)
            outgoing[2 * (mask % 2) + mask // 2] = piece
        pieces = jnp.take(jnp.stack(outgoing), block_order, axis=0)
        return pieces.reshape(total_tokens, local_cols)

    def plane_scale(square_sum):
        scale = lax.rsqrt(square_sum / D + epsilon)
        scale = [scale] + [across_plane(scale, mask) for mask in (2, 1, 3)]
        scale = jnp.concatenate(scale, axis=1)
        return jnp.sum(selector.astype(f32) * scale, axis=1, keepdims=True)

    def rows_of(span, near, far, row_scale):
        pieces = (near, far, across(near, 0), across(far, 0))
        return select_rows(span, selector, row_scale, ffn_gain, pieces)

    if not exact:
        row_scale = plane_scale(lax.psum(squares, "mp", axis_index_groups=groups))
        near = jnp.stack(from_planes(attended_here, plane, planes))
        near = jnp.take(near, (jnp.arange(planes, dtype=jnp.int32) - plane) % planes, axis=0)
        near = near.reshape(EXPERTS, planes // EXPERTS, block, QUAD * local_cols)
        near = near.transpose(0, 2, 1, 3).reshape(EXPERTS, block, -1)
        hidden = ()
        for span in range(EXPERTS):
            rows = rows_of(jnp.int32(span), near[span], across(near[span], 1), row_scale)
            last = span == EXPERTS - 1
            hidden = hidden_part(jnp.int32(span), rows, w_gate, w_up, hidden, last)
        activated = hidden[0]
        attended = own_columns()
        total = wide_dot(activated, w_down)
        incoming = lax.all_to_all(
            total.reshape(CAP, -1, local_cols), "mp", split_axis=1, concat_axis=1, tiled=True
        )
        summed = jnp.sum(incoming.reshape(CAP, EXPERTS, -1, local_cols), axis=2)
        summed = summed.reshape(CAP * EXPERTS, local_cols)
        code_row = jnp.arange(CAP * EXPERTS, dtype=jnp.int32)[None, :]
        slot_codes = slots * EXPERTS + routes
        weighting = sum(
            gates[:, k : k + 1] * (slot_codes[:, k : k + 1] == code_row).astype(f32) for k in range(2)
        )
        mixed = jnp.dot(weighting, summed, precision=lax.Precision.HIGHEST)
        return (attended, mixed.astype(bf16))

    def span(step):
        return (plane + step) % planes

    near, far = {0: attended_here}, {}
    square_sum = squares
    for step in range(1, planes):
        square_sum = square_sum + to_plane(squares, step)
    near[1] = to_plane(near[0], -1)
    far[0] = across(near[0], 1)
    row_scale = plane_scale(square_sum)
    near[0], far[0], near[1], row_scale = stage(near[0], far[0], near[1], row_scale)

    near[2] = to_plane(near[0], -2)
    far[1] = across(near[1], 1)
    rows = rows_of(span(0), near[0], far[0], row_scale)
    hidden, mark = hidden_part(span(0), rows, w_gate, w_up, (), False)
    near[0], near[1], far[1], near[2], row_scale, mark = stage(
        near[0], near[1], far[1], near[2], row_scale, mark
    )

    near[3] = to_plane(near[0], -3)
    far[2] = across(near[2], 1)
    rows = rows_of(span(1), near[1], far[1], row_scale)
    hidden, mark = hidden_part(span(1), rows, w_gate, w_up, (hidden, mark), False)
    near[2], far[2], near[3], row_scale, mark = stage(near[2], far[2], near[3], row_scale, mark)

    far[3] = across(near[3], 1)
    rows = rows_of(span(2), near[2], far[2], row_scale)
    hidden, mark = hidden_part(span(2), rows, w_gate, w_up, (hidden, mark), False)
    near[3], far[3], row_scale, mark = stage(near[3], far[3], row_scale, mark)

    rows = rows_of(span(3), near[3], far[3], row_scale)
    activated, peak = hidden_part(span(3), rows, w_gate, w_up, (hidden, mark), True)
    activated, peak, slots, routes, attended_here = stage(
        activated, peak, slots, routes, attended_here
    )

    bound = 0.0625 * QUAD * activated.shape[1] / 32768.0

    def parts_of(*wanted, peak=None):
        blocks = [2 * span(step) + (1 - side if kind == "away" else side) for kind, step in wanted]
        return down_parts(blocks, core, activated, w_down, local_cols, peak)

    def chip_sum(part):
        return part[1] + across(part[0], 0)

    def outward(total, exponent, marked):
        total = (total * jnp.exp2(-exponent)).astype(jnp.float16)
        if not marked:
            return total
        exponent = jnp.broadcast_to(exponent.astype(jnp.float16), (16, local_cols))
        return jnp.concatenate([total, exponent], axis=0)

    def exponent_of(came):
        return came[CAP, 0].astype(f32)

    def mix_of(step, result, exponent):
        source = (plane - step) % planes
        code = jnp.where(routes == source, slots, -1)
        code_row = jnp.arange(CAP, dtype=jnp.int32)[None, :]
        placing = ((code[:, 0:1] == code_row) | (code[:, 1:2] == code_row)).astype(bf16)
        result = result[:CAP].astype(f32) * jnp.exp2(exponent)
        high = result.astype(bf16)
        low = (result - high.astype(f32)).astype(bf16)
        return wide_dot(placing, high) + wide_dot(placing, low)

    (away_2,) = parts_of(("away", 2), peak=peak)
    attended = own_columns()
    activated, peak, attended, *away_2 = stage(activated, peak, attended, *away_2)

    came = across(away_2[0], 0)
    peak = jnp.maximum(jnp.max(peak), came[CAP, 0])
    exponent = jnp.ceil(jnp.log2(jnp.maximum(peak * bound, 1e-30)))
    sent_2 = outward(away_2[1] + came[:CAP], exponent, True)
    away_1, near_2 = parts_of(("away", 1), ("near", 2))
    activated, exponent, sent_2, *parts = stage(activated, exponent, sent_2, *away_1, *near_2)

    came_2 = across(sent_2, 1)
    sent_1, total_2 = outward(chip_sum(parts[:2]), exponent, False), chip_sum(parts[2:])
    away_3, away_0, near_1 = parts_of(("away", 3), ("away", 0), ("near", 1))
    activated, exponent, came_2, sent_1, total_2, *parts = stage(
        activated, exponent, came_2, sent_1, total_2, *away_3, *away_0, *near_1
    )

    there = exponent_of(came_2)
    common = jnp.maximum(exponent, there)

    def finished(total, came, marked=True):
        total = (total + came[:CAP].astype(f32) * jnp.exp2(there)) * slot_gate
        return outward(total, common, marked)

    result_2 = to_plane(finished(total_2, came_2), 2)
    came_1 = across(sent_1, 1)
    sent_3 = outward(chip_sum(parts[:2]), exponent, False)
    sent_0 = outward(chip_sum(parts[2:4]), exponent, False)
    total_1 = chip_sum(parts[4:])
    came_3 = across(sent_3, 1)
    near_3, near_0 = parts_of(("near", 3), ("near", 0))
    result_2, came_1, came_3, sent_0, total_1, there, common, *parts = stage(
        result_2, came_1, came_3, sent_0, total_1, there, common, *near_3, *near_0
    )

    result_1 = to_plane(finished(total_1, came_1), 1)
    came_0 = across(sent_0, 1)
    result_3 = to_plane(finished(chip_sum(parts[:2]), came_3), 3)
    total_0 = chip_sum(parts[2:])
    mixed = mix_of(2, result_2, exponent_of(result_2))
    result_1, result_3, total_0, came_0, there, common, mixed = stage(
        result_1, result_3, total_0, came_0, there, common, mixed
    )
    mixed = mixed + mix_of(1, result_1, exponent_of(result_1))
    mixed = mixed + mix_of(3, result_3, exponent_of(result_3))
    mixed = mixed + mix_of(0, finished(total_0, came_0, False), common)
    return (attended, mixed.astype(bf16))


def solution(mesh):
    placed = (
        P("groups", "mp"),
        P(("groups", "mp")),
        P(("groups", "mp"), None),
        P(("groups", "mp"), None),
        P("groups", "mp"),
        P("groups", "mp"),
        P("groups", "mp"),
        P("groups"),
        P("groups", None),
        P("groups", None),
        P("groups", None),
        P("groups", "mp"),
        P("groups", "mp"),
        P(("groups", "mp"), None),
    )
    return jax.shard_map(
        body,
        mesh=mesh,
        in_specs=placed,
        out_specs=(P("groups", "mp"), P("groups", "mp")),
        check_vma=False,
    )
```

time: 661 us -> 266 us (0.40)
  waiting for transfers between devices: 365 us -> 47.4 us
  blocking collectives: 168 us -> 0 us
  Pallas kernels: 0 us -> 70.4 us
  matrix products: 80.1 us -> 12.5 us
  starting transfers between devices: 8.4 us -> 66.6 us
  local copies, waits for them, and re-layouts: 16.9 us -> 37.2 us
  other arithmetic: 8.02 us -> 21.6 us
  between operations: 14.4 us -> 6.24 us
    all_to_all x1 -> x0, waiting for transfers between devices: 239 us -> none  [body(): lax.all_to_all(partial_value.reshape(CAP, devices, local_cols), 'mp', spl...]
    all_to_all x1 -> x0, blocking collectives: 128 us -> none  [body(): lax.all_to_all(outgoing, 'mp', split_axis=1, concat_axis=1, tiled=True)]
    pallas_call x0 -> x12, Pallas kernels: none -> 70.4 us  [the longest x4 36.2 us: hidden_part(): pl.pallas_call(functools.partial(hidden_kernel, first, last), grid_spec=p...]
    dot_general x11 -> x16, matrix products: 80.1 us -> 12.5 us  [wide_dot(): return jnp.dot(a, b, preferred_element_type=f32)]
    ppermute x4 -> x61, starting transfers between devices: 2.42 us -> 66.6 us  [the longest x18 25.2 us: to_plane(): lax.ppermute(array, 'mp', [(i, (i + QUAD * step) % n) for i in range(n)])]
    psum x1 -> x0, waiting for transfers between devices: 64.1 us -> none  [body(): square_sum, latent_total = lax.psum((square_part, latent_part), 'mp')]
    reduce_scatter x1 -> x0, waiting for transfers between devices: 60.3 us -> none  [body(): lax.psum_scatter(query_terms.reshape(head_count * total_tokens, HD), 'mp'...]
    ppermute x4 -> x61, waiting for transfers between devices: 1.57 us -> 47.4 us  [the longest x31 28.1 us: across(): lax.ppermute(array, 'mp', [(i, i ^ 1 << bit) for i in range(lax.axis_size...]
  transfers between devices with their start and end apart: 7 -> 61, of which waited for: 4 -> 18; matrix products, arithmetic and copies ran while one was open for 1% -> 11% of each run, Pallas kernels for 0% -> 23%
where the time goes in v1:
time: 266 us; the launch traced here: 262 us
  Pallas kernels  70.4 us (26%)
  starting transfers between devices  66.6 us (25%)
  waiting for transfers between devices  47.4 us (18%)
  local copies, waits for them, and re-layouts  37.2 us (14%)
  other arithmetic  21.6 us (8%)
  matrix products  12.5 us (5%)
  between operations  6.24 us (2%)
    pallas_call x4, Pallas kernels, hidden_part(): pl.pallas_call(functools.partial(hidden_kernel, first, last), grid_spec=p...  36.2 us
    ppermute x31, waiting for transfers between devices, across(): lax.ppermute(array, 'mp', [(i, i ^ 1 << bit) for i in range(lax.axis_size...  28.1 us
    pallas_call x4, Pallas kernels, down_parts(): pl.pallas_call(functools.partial(down_kernel, count, marked), grid_spec=p...  27.5 us
    ppermute x18, starting transfers between devices, to_plane(): lax.ppermute(array, 'mp', [(i, (i + QUAD * step) % n) for i in range(n)])  25.2 us
    unnamed x73, local copies, waits for them, and re-layouts  23.7 us
    ppermute x31, starting transfers between devices, across(): lax.ppermute(array, 'mp', [(i, i ^ 1 << bit) for i in range(lax.axis_size...  21.8 us
    ppermute x12, starting transfers between devices, across_plane(): lax.ppermute(array, 'mp', [(i, i ^ mask) for i in range(lax.axis_size('mp...  19.7 us
    ppermute x18, waiting for transfers between devices, to_plane(): lax.ppermute(array, 'mp', [(i, (i + QUAD * step) % n) for i in range(n)])  14.6 us
  transfers between devices with their start and end apart: 61, of which 18 were waited for; matrix products, arithmetic and copies ran while one was open for 11% of the time, Pallas kernels for 23%

profile of v1, /device:TPU:13, one launch (start us, length us, event | category | flops | bytes accessed | tf_op | source)
XLA Modules:
  0.0 262.0 jit_solution(2073755683344202501)
XLA Ops:
  8.8 12.3 %collective-permute-done.1 = f32[136,1024]{1,0:T(8,128)S(1)} collective-permute-done((f32[136,1024]{1,0:T(8,128)S(1)}, f32[136,1024]{1,0:T(8,128)S(1)}, u32[]{:S(2)}, u32[]{:S(2)}) %collective-permute-start.1) | collective-permute-done | bytes 557088 | tf_op jit(solution)/shard_map/ppermute | solution.py:24
  25.2 2.1 collective-permute-start.5
  27.5 6.6 %collective-permute-start.7 = (bf16[64,512]{1,0:T(8,128)(2,1)S(1)}, bf16[64,512]{1,0:T(8,128)(2,1)S(1)}, u32[]{:S(2)}, u32[]{:S(2)}) collective-permute-start(bf16[64,512]{1,0:T(8,128)(2,1)S(1)} %pad_maximum_fusion.7), channel_id=1, source_target_pairs={{0,3},{1,2},{2,1},{3,0},{4,7},{5,6},{6,5},{7,4},{8,11},{9,10},{10,... | collective-permute-start | bytes 196616 | tf_op jit(solution)/shard_map/ppermute | solution.py:28
  42.7 2.6 %collective-permute-start.21 = (bf16[128,384]{1,0:T(8,128)(2,1)S(1)}, bf16[128,384]{1,0:T(8,128)(2,1)S(1)}, u32[]{:S(2)}, u32[]{:S(2)}) collective-permute-start(bf16[128,384]{1,0:T(8,128)(2,1)S(1)} %get-tuple-element.178), channel_id=1, source_target_pairs={{0,3},{1,2},{2,1},{3,0},{4,7},{5,6},{6,5},{7,4},{8,11},{9,10},{10,... | collective-permute-start | bytes 294920 | tf_op jit(solution)/shard_map/ppermute | solution.py:28
  45.4 4.2 %collective-permute-done.11 = bf16[512,384]{1,0:T(8,128)(2,1)S(1)} collective-permute-done((bf16[512,384]{1,0:T(8,128)(2,1)S(1)}, bf16[512,384]{1,0:T(8,128)(2,1)S(1)}, u32[]{:S(2)}, u32[]{:S(2)}) %collective-permute-start.11) | collective-permute-done | bytes 393248 | tf_op jit(solution)/shard_map/ppermute | solution.py:24
  49.6 4.1 %collective-permute-start.13 = (bf16[512,384]{1,0:T(8,128)(2,1)S(1)}, bf16[512,384]{1,0:T(8,128)(2,1)S(1)}, u32[]{:S(2)}, u32[]{:S(2)}) collective-permute-start(bf16[512,384]{1,0:T(8,128)(2,1)S(1)} %fusion.48), channel_id=1, source_target_pairs={{0,1},{1,0},{2,3},{3,2},{4,5},{5,4},{6,7},{7,6},{8,9},{9,8},{10,11... | collective-permute-start | bytes 1179656 | tf_op jit(solution)/shard_map/ppermute | solution.py:24
  62.2 2.1 collective-permute-start.18
  65.5 1.9 gather_fusion.2
  72.0 2.1 multiply_reduce_fusion.1
  79.9 2.9 %collective-permute-start.28 = (f32[1,128]{1,0:T(1,128)S(1)}, f32[1,128]{1,0:T(1,128)S(1)}, u32[]{:S(2)}, u32[]{:S(2)}) collective-permute-start(f32[1,128]{1,0:T(1,128)S(1)} %add_rsqrt_fusion), channel_id=1, source_target_pairs={{0,1},{1,0},{2,3},{3,2},{4,5},{5,4},{6,7},{7,6},{8,9},{9,8},{10,11... | collective-permute-start | bytes 1544 | tf_op jit(solution)/shard_map/ppermute | solution.py:28
  85.5 2.6 collective-permute-done.29
  89.3 3.0 %collective-permute-start.31 = (bf16[128,1536]{1,0:T(8,128)(2,1)S(1)}, bf16[128,1536]{1,0:T(8,128)(2,1)S(1)}, u32[]{:S(2)}, u32[]{:S(2)}) collective-permute-start(bf16[128,1536]{1,0:T(8,128)(2,1)S(1)} %get-tuple-element.212.a_ref), channel_id=1, source_target_pairs={{0,8},{1,9},{2,10},{3,11},{4,12},{5,13},{6,14},{7,15},{8,0},{9,1},... | collective-permute-start | bytes 1179656 | tf_op jit(solution)/shard_map/ppermute | solution.py:33
  95.0 8.7 %shard_map.150 = (f32[2,448,2048]{2,1,0:T(8,128)S(1)}, f32[8,128]{1,0:T(8,128)S(1)}) custom-call(s32[1]{0:T(128)} %bitcast.41.where_ref, bf16[448,1536]{1,0:T(8,128)(2,1)S(1)} %shard_map.149.rows_ref, bf16[6144,2048]{1,0:T(8,128)(2,1)} %gate_ref.7, bf16[6144,2048]{1,0:T(8,128)(2,1)} %up_ref.7), custom_call_target="tpu_custom_call" | custom-call | flops 5637144576 | bytes 12582912 | tf_op jit(solution)/shard_map/pallas_call | solution.py:128
  103.7 3.0 %copy-done.2 = f32[2,448,2048]{2,1,0:T(8,128)} copy-done((f32[2,448,2048]{2,1,0:T(8,128)}, f32[2,448,2048]{2,1,0:T(8,128)S(1)}, u32[]{:S(2)}) %copy-start.2) | copy-done | bytes 7340056
  110.6 2.0 shard_map.151.rows_ref
  112.6 3.1 %copy-done.3 = f32[2,448,2048]{2,1,0:T(8,128)S(1)} copy-done((f32[2,448,2048]{2,1,0:T(8,128)S(1)}, f32[2,448,2048]{2,1,0:T(8,128)}, u32[]{:S(2)}) %copy-start.3) | copy-done | bytes 7340056
  115.7 9.0 %shard_map.152 = (f32[2,448,2048]{2,1,0:T(8,128)S(1)}, f32[8,128]{1,0:T(8,128)S(1)}) custom-call(s32[1]{0:T(128)} %bitcast.43.where_ref, bf16[448,1536]{1,0:T(8,128)(2,1)S(1)} %shard_map.151.rows_ref, bf16[6144,2048]{1,0:T(8,128)(2,1)} %gate_ref.7, bf16[6144,2048]{1,0:T(8,128)(2,1)} %up_ref.7, ...), custom_call_target="tpu_custom_call", output_to_operand_aliasing={{0}: (4, {})} | custom-call | flops 5637144576 | bytes 12582912 | tf_op jit(solution)/shard_map/pallas_call | solution.py:128
  124.7 3.0 %copy-done.4 = f32[2,448,2048]{2,1,0:T(8,128)} copy-done((f32[2,448,2048]{2,1,0:T(8,128)}, f32[2,448,2048]{2,1,0:T(8,128)S(1)}, u32[]{:S(2)}) %copy-start.4) | copy-done | bytes 7340056
  132.7 3.1 %copy-done.5 = f32[2,448,2048]{2,1,0:T(8,128)S(1)} copy-done((f32[2,448,2048]{2,1,0:T(8,128)S(1)}, f32[2,448,2048]{2,1,0:T(8,128)}, u32[]{:S(2)}) %copy-start.5) | copy-done | bytes 7340056
  135.8 9.1 %shard_map.154 = (f32[2,448,2048]{2,1,0:T(8,128)S(1)}, f32[8,128]{1,0:T(8,128)S(1)}) custom-call(s32[1]{0:T(128)} %bitcast.44.where_ref, bf16[448,1536]{1,0:T(8,128)(2,1)S(1)} %shard_map.153.rows_ref, bf16[6144,2048]{1,0:T(8,128)(2,1)} %gate_ref.7, bf16[6144,2048]{1,0:T(8,128)(2,1)} %up_ref.7, ...), custom_call_target="tpu_custom_call", output_to_operand_aliasing={{0}: (4, {})} | custom-call | flops 5637144576 | bytes 12582912 | tf_op jit(solution)/shard_map/pallas_call | solution.py:128
  144.9 3.0 %copy-done.6 = f32[2,448,2048]{2,1,0:T(8,128)} copy-done((f32[2,448,2048]{2,1,0:T(8,128)}, f32[2,448,2048]{2,1,0:T(8,128)S(1)}, u32[]{:S(2)}) %copy-start.6) | copy-done | bytes 7340056
  151.0 3.1 %copy-done.7 = f32[2,448,2048]{2,1,0:T(8,128)S(1)} copy-done((f32[2,448,2048]{2,1,0:T(8,128)S(1)}, f32[2,448,2048]{2,1,0:T(8,128)}, u32[]{:S(2)}) %copy-start.7) | copy-done | bytes 7340056
  154.1 9.4 %shard_map.156 = (bf16[448,2048]{1,0:T(8,128)(2,1)S(1)}, f32[8,128]{1,0:T(8,128)S(1)}) custom-call(s32[1]{0:T(128)} %bitcast.where_ref, bf16[448,1536]{1,0:T(8,128)(2,1)S(1)} %shard_map.155.rows_ref, bf16[6144,2048]{1,0:T(8,128)(2,1)} %gate_ref.7, bf16[6144,2048]{1,0:T(8,128)(2,1)} %up_ref.7, f32[2,448,2048]{2,1,0:T(8,128)S(1)} %copy-done.7, ...), custom_call_target="tpu_custom_call" | custom-call | flops 5637144576 | bytes 12582912 | tf_op jit(solution)/shard_map/pallas_call | solution.py:128
  165.7 4.9 %shard_map.157 = (f32[456,384]{1,0:T(8,128)}, f32[448,384]{1,0:T(8,128)S(1)}) custom-call(s32[2]{0:T(128)S(1)} %pad_add_fusion.where_ref, bf16[448,2048]{1,0:T(8,128)(2,1)S(1)} %get-tuple-element.248.act_ref, bf16[2048,6144]{1,0:T(8,128)(2,1)} %w_ref.7, f32[8,128]{1,0:T(8,128)S(1)} %get-tuple-element.217.refs_0_), custom_call_target="tpu_custom_call" | custom-call | flops 1409286144 | bytes 3145728 | tf_op jit(solution)/shard_map/pallas_call | solution.py:174
  173.3 7.0 %shard_map.158 = (f32[448,384]{1,0:T(8,128)}, f32[448,384]{1,0:T(8,128)S(1)}, f32[448,384]{1,0:T(8,128)}, f32[448,384]{1,0:T(8,128)S(1)}) custom-call(s32[3]{0:T(128)S(1)} %get-tuple-element.328.where_ref, bf16[448,2048]{1,0:T(8,128)(2,1)S(1)} %get-tuple-element.248.act_ref, bf16[2048,6144]{1,0:T(8,128)(2,1)} %w_ref.7), custom_call_target="tpu_custom_call" | custom-call | flops 2818572288 | bytes 6291456 | tf_op jit(solution)/shard_map/pallas_call | solution.py:174
  188.2 8.7 %shard_map.159 = (f32[448,384]{1,0:T(8,128)}, f32[448,384]{1,0:T(8,128)S(1)}, f32[448,384]{1,0:T(8,128)S(1)}, f32[448,384]{1,0:T(8,128)S(1)}, f32[448,384]{1,0:T(8,128)S(1)}, /*index=5*/f32[448,384]{1,0:T(8,128)S(1)}) custom-call(s32[4]{0:T(128)S(1)} %pad_add_fusion.1.where_ref, bf16[448,2048]{1,0:T(8,128)(2,1)S(1)} %get-tuple-element.248.act_ref, ...), custom_call_target="tpu_custom_call" | custom-call | flops 4227858432 | bytes 9437184 | tf_op jit(solution)/shard_map/pallas_call | solution.py:174
  199.4 2.3 add.449
  208.1 4.0 %collective-permute-start.50 = (f16[464,384]{1,0:T(8,128)(2,1)S(1)}, f16[464,384]{1,0:T(8,128)(2,1)S(1)}, u32[]{:S(2)}, u32[]{:S(2)}) collective-permute-start(f16[464,384]{1,0:T(8,128)(2,1)S(1)} %concatenate.89), channel_id=1, source_target_pairs={{0,8},{1,9},{2,10},{3,11},{4,12},{5,13},{6,14},{7,15},{8,0},{9,1},... | collective-permute-start | bytes 1069064 | tf_op jit(solution)/shard_map/ppermute | solution.py:33
  214.8 7.0 %shard_map.160 = (f32[448,384]{1,0:T(8,128)}, f32[448,384]{1,0:T(8,128)S(1)}, f32[448,384]{1,0:T(8,128)S(1)}, f32[448,384]{1,0:T(8,128)S(1)}) custom-call(s32[3]{0:T(128)S(1)} %get-tuple-element.329.where_ref, bf16[448,2048]{1,0:T(8,128)(2,1)S(1)} %get-tuple-element.248.act_ref, bf16[2048,6144]{1,0:T(8,128)(2,1)} %w_ref.7), custom_call_target="tpu_custom_call" | custom-call | flops 2818572288 | bytes 6291456 | tf_op jit(solution)/shard_map/pallas_call | solution.py:174
  238.0 4.1 %collective-permute-done.60 = f16[448,384]{1,0:T(8,128)(2,1)S(1)} collective-permute-done((f16[448,384]{1,0:T(8,128)(2,1)S(1)}, f16[448,384]{1,0:T(8,128)(2,1)S(1)}, u32[]{:S(2)}, u32[]{:S(2)}) %collective-permute-start.60) | collective-permute-done | bytes 344096 | tf_op jit(solution)/shard_map/ppermute | solution.py:24
  242.1 2.5 collective-permute-done.58
  244.6 7.6 %collective-permute-done.56 = f16[464,384]{1,0:T(8,128)(2,1)} collective-permute-done((f16[464,384]{1,0:T(8,128)(2,1)S(1)}, f16[464,384]{1,0:T(8,128)(2,1)}, u32[]{:S(2)}, u32[]{:S(2)}) %collective-permute-start.56) | collective-permute-done | bytes 356384 | tf_op jit(solution)/shard_map/ppermute | solution.py:33
  (288 shorter events, 104.8 us)
Async XLA Ops:
  7.2 13.9 %collective-permute-start.1 = (f32[136,1024]{1,0:T(8,128)S(1)}, f32[136,1024]{1,0:T(8,128)S(1)}, u32[]{:S(2)}, u32[]{:S(2)}) collective-permute-start(f32[136,1024]{1,0:T(8,128)S(1)} %select_maximum_fusion.1), channel_id=1, source_target_pairs={{0,2},{1,3},{2,0},{3,1},{4,6},{5,7},{6,4},{7,5},{8,10},{9,11},{10,... | collective-permute-start | bytes 1671176 | tf_op jit(solution)/shard_map/ppermute | solution.py:24
  22.7 11.5 %collective-permute-start.3 = (f32[136,256]{1,0:T(8,128)S(1)}, f32[136,256]{1,0:T(8,128)S(1)}, u32[]{:S(2)}, u32[]{:S(2)}) collective-permute-start(f32[136,256]{1,0:T(8,128)S(1)} %get-tuple-element.318), channel_id=1, source_target_pairs={{0,8},{1,9},{2,10},{3,11},{4,12},{5,13},{6,14},{7,15},{8,0},{9,1},... | collective-permute-start | bytes 417800 | tf_op jit(solution)/shard_map/ppermute | solution.py:33
  23.8 13.0 %collective-permute-start.4 = (f32[136,256]{1,0:T(8,128)S(1)}, f32[136,256]{1,0:T(8,128)S(1)}, u32[]{:S(2)}, u32[]{:S(2)}) collective-permute-start(f32[136,256]{1,0:T(8,128)S(1)} %get-tuple-element.319), channel_id=1, source_target_pairs={{0,12},{1,13},{2,14},{3,15},{4,0},{5,1},{6,2},{7,3},{8,4},{9,5},{1... | collective-permute-start | bytes 417800 | tf_op jit(solution)/shard_map/ppermute | solution.py:33
  25.2 11.8 %collective-permute-start.5 = (bf16[64,512]{1,0:T(8,128)(2,1)S(1)}, bf16[64,512]{1,0:T(8,128)(2,1)S(1)}, u32[]{:S(2)}, u32[]{:S(2)}) collective-permute-start(bf16[64,512]{1,0:T(8,128)(2,1)S(1)} %pad_maximum_fusion.7), channel_id=1, source_target_pairs={{0,1},{1,0},{2,3},{3,2},{4,5},{5,4},{6,7},{7,6},{8,9},{9,8},{10,11... | collective-permute-start | bytes 196616 | tf_op jit(solution)/shard_map/ppermute | solution.py:28
  27.3 9.7 %collective-permute-start.6 = (bf16[64,512]{1,0:T(8,128)(2,1)S(1)}, bf16[64,512]{1,0:T(8,128)(2,1)S(1)}, u32[]{:S(2)}, u32[]{:S(2)}) collective-permute-start(bf16[64,512]{1,0:T(8,128)(2,1)S(1)} %pad_maximum_fusion.7), channel_id=1, source_target_pairs={{0,2},{1,3},{2,0},{3,1},{4,6},{5,7},{6,4},{7,5},{8,10},{9,11},{10,... | collective-permute-start | bytes 196616 | tf_op jit(solution)/shard_map/ppermute | solution.py:28
  27.5 9.4 %collective-permute-start.7 = (bf16[64,512]{1,0:T(8,128)(2,1)S(1)}, bf16[64,512]{1,0:T(8,128)(2,1)S(1)}, u32[]{:S(2)}, u32[]{:S(2)}) collective-permute-start(bf16[64,512]{1,0:T(8,128)(2,1)S(1)} %pad_maximum_fusion.7), channel_id=1, source_target_pairs={{0,3},{1,2},{2,1},{3,0},{4,7},{5,6},{6,5},{7,4},{8,11},{9,10},{10,... | collective-permute-start | bytes 196616 | tf_op jit(solution)/shard_map/ppermute | solution.py:28
  34.1 19.8 %collective-permute-start.19 = (bf16[128,384]{1,0:T(8,128)(2,1)S(1)}, bf16[128,384]{1,0:T(8,128)(2,1)S(1)}, u32[]{:S(2)}, u32[]{:S(2)}) collective-permute-start(bf16[128,384]{1,0:T(8,128)(2,1)S(1)} %get-tuple-element.176), channel_id=1, source_target_pairs={{0,1},{1,0},{2,3},{3,2},{4,5},{5,4},{6,7},{7,6},{8,9},{9,8},{10,11... | collective-permute-start | bytes 294920 | tf_op jit(solution)/shard_map/ppermute | solution.py:28
  40.3 9.3 %collective-permute-start.11 = (bf16[512,384]{1,0:T(8,128)(2,1)S(1)}, bf16[512,384]{1,0:T(8,128)(2,1)S(1)}, u32[]{:S(2)}, u32[]{:S(2)}) collective-permute-start(bf16[512,384]{1,0:T(8,128)(2,1)S(1)} %fusion.48), channel_id=1, source_target_pairs={{0,2},{1,3},{2,0},{3,1},{4,6},{5,7},{6,4},{7,5},{8,10},{9,11},{10,... | collective-permute-start | bytes 1179656 | tf_op jit(solution)/shard_map/ppermute | solution.py:24
  42.4 12.4 %collective-permute-start.20 = (bf16[128,384]{1,0:T(8,128)(2,1)S(1)}, bf16[128,384]{1,0:T(8,128)(2,1)S(1)}, u32[]{:S(2)}, u32[]{:S(2)}) collective-permute-start(bf16[128,384]{1,0:T(8,128)(2,1)S(1)} %get-tuple-element.177), channel_id=1, source_target_pairs={{0,2},{1,3},{2,0},{3,1},{4,6},{5,7},{6,4},{7,5},{8,10},{9,11},{10,... | collective-permute-start | bytes 294920 | tf_op jit(solution)/shard_map/ppermute | solution.py:28
  42.7 12.7 %collective-permute-start.21 = (bf16[128,384]{1,0:T(8,128)(2,1)S(1)}, bf16[128,384]{1,0:T(8,128)(2,1)S(1)}, u32[]{:S(2)}, u32[]{:S(2)}) collective-permute-start(bf16[128,384]{1,0:T(8,128)(2,1)S(1)} %get-tuple-element.178), channel_id=1, source_target_pairs={{0,3},{1,2},{2,1},{3,0},{4,7},{5,6},{6,5},{7,4},{8,11},{9,10},{10,... | collective-permute-start | bytes 294920 | tf_op jit(solution)/shard_map/ppermute | solution.py:28
  60.6 11.3 %collective-permute-start.16 = (bf16[128,128]{1,0:T(8,128)(2,1)S(1)}, bf16[128,128]{1,0:T(8,128)(2,1)S(1)}, u32[]{:S(2)}, u32[]{:S(2)}) collective-permute-start(bf16[128,128]{1,0:T(8,128)(2,1)S(1)} %convolution_convert_fusion.1), channel_id=1, source_target_pairs={{0,12},{1,13},{2,14},{3,15},{4,0},{5,1},{6,2},{7,3},{8,4},{9,5},{1... | collective-permute-start | bytes 98312 | tf_op jit(solution)/shard_map/ppermute | solution.py:33
  62.2 9.8 %collective-permute-start.17 = (bf16[128,128]{1,0:T(8,128)(2,1)S(1)}, bf16[128,128]{1,0:T(8,128)(2,1)S(1)}, u32[]{:S(2)}, u32[]{:S(2)}) collective-permute-start(bf16[128,128]{1,0:T(8,128)(2,1)S(1)} %convolution_convert_fusion.1), channel_id=1, source_target_pairs={{0,8},{1,9},{2,10},{3,11},{4,12},{5,13},{6,14},{7,15},{8,0},{9,1},... | collective-permute-start | bytes 98312 | tf_op jit(solution)/shard_map/ppermute | solution.py:33
  62.2 9.8 %collective-permute-start.18 = (bf16[128,128]{1,0:T(8,128)(2,1)S(1)}, bf16[128,128]{1,0:T(8,128)(2,1)S(1)}, u32[]{:S(2)}, u32[]{:S(2)}) collective-permute-start(bf16[128,128]{1,0:T(8,128)(2,1)S(1)} %convolution_convert_fusion.1), channel_id=1, source_target_pairs={{0,4},{1,5},{2,6},{3,7},{4,8},{5,9},{6,10},{7,11},{8,12},{9,13},{1... | collective-permute-start | bytes 98312 | tf_op jit(solution)/shard_map/ppermute | solution.py:33
  76.9 11.3 %collective-permute-start.22 = (bf16[128,1536]{1,0:T(8,128)(2,1)S(1)}, bf16[128,1536]{1,0:T(8,128)(2,1)S(1)}, u32[]{:S(2)}, u32[]{:S(2)}) collective-permute-start(bf16[128,1536]{1,0:T(8,128)(2,1)S(1)} %get-tuple-element.212.a_ref), channel_id=1, source_target_pairs={{0,2},{1,3},{2,0},{3,1},{4,6},{5,7},{6,4},{7,5},{8,10},{9,11},{10,... | collective-permute-start | bytes 1179656 | tf_op jit(solution)/shard_map/ppermute | solution.py:24
  77.7 10.5 %collective-permute-start.23 = (bf16[128,1536]{1,0:T(8,128)(2,1)S(1)}, bf16[128,1536]{1,0:T(8,128)(2,1)S(1)}, u32[]{:S(2)}, u32[]{:S(2)}) collective-permute-start(bf16[128,1536]{1,0:T(8,128)(2,1)S(1)} %get-tuple-element.212.a_ref), channel_id=1, source_target_pairs={{0,12},{1,13},{2,14},{3,15},{4,0},{5,1},{6,2},{7,3},{8,4},{9,5},{1... | collective-permute-start | bytes 1179656 | tf_op jit(solution)/shard_map/ppermute | solution.py:33
  89.3 18.7 %collective-permute-start.31 = (bf16[128,1536]{1,0:T(8,128)(2,1)S(1)}, bf16[128,1536]{1,0:T(8,128)(2,1)S(1)}, u32[]{:S(2)}, u32[]{:S(2)}) collective-permute-start(bf16[128,1536]{1,0:T(8,128)(2,1)S(1)} %get-tuple-element.212.a_ref), channel_id=1, source_target_pairs={{0,8},{1,9},{2,10},{3,11},{4,12},{5,13},{6,14},{7,15},{8,0},{9,1},... | collective-permute-start | bytes 1179656 | tf_op jit(solution)/shard_map/ppermute | solution.py:33
  92.4 14.2 %collective-permute-start.30 = (bf16[128,1536]{1,0:T(8,128)(2,1)S(1)}, bf16[128,1536]{1,0:T(8,128)(2,1)S(1)}, u32[]{:S(2)}, u32[]{:S(2)}) collective-permute-start(bf16[128,1536]{1,0:T(8,128)(2,1)S(1)} %collective-permute-done.23.a_ref), channel_id=1, source_target_pairs={{0,2},{1,3},{2,0},{3,1},{4,6},{5,7},{6,4},{7,5},{8,10},{9,11},{10,... | collective-permute-start | bytes 1179656 | tf_op jit(solution)/shard_map/ppermute | solution.py:24
  108.6 19.0 %collective-permute-start.34 = (bf16[128,1536]{1,0:T(8,128)(2,1)S(1)}, bf16[128,1536]{1,0:T(8,128)(2,1)S(1)}, u32[]{:S(2)}, u32[]{:S(2)}) collective-permute-start(bf16[128,1536]{1,0:T(8,128)(2,1)S(1)} %collective-permute-done.31.a_ref), channel_id=1, source_target_pairs={{0,2},{1,3},{2,0},{3,1},{4,6},{5,7},{6,4},{7,5},{8,10},{9,11},{10,... | collective-permute-start | bytes 1179656 | tf_op jit(solution)/shard_map/ppermute | solution.py:24
  109.1 18.6 %collective-permute-start.35 = (bf16[128,1536]{1,0:T(8,128)(2,1)S(1)}, bf16[128,1536]{1,0:T(8,128)(2,1)S(1)}, u32[]{:S(2)}, u32[]{:S(2)}) collective-permute-start(bf16[128,1536]{1,0:T(8,128)(2,1)S(1)} %get-tuple-element.212.a_ref), channel_id=1, source_target_pairs={{0,4},{1,5},{2,6},{3,7},{4,8},{5,9},{6,10},{7,11},{8,12},{9,13},{1... | collective-permute-start | bytes 1179656 | tf_op jit(solution)/shard_map/ppermute | solution.py:33
  129.0 18.9 %collective-permute-start.38 = (bf16[128,1536]{1,0:T(8,128)(2,1)S(1)}, bf16[128,1536]{1,0:T(8,128)(2,1)S(1)}, u32[]{:S(2)}, u32[]{:S(2)}) collective-permute-start(bf16[128,1536]{1,0:T(8,128)(2,1)S(1)} %collective-permute-done.35.a_ref), channel_id=1, source_target_pairs={{0,2},{1,3},{2,0},{3,1},{4,6},{5,7},{6,4},{7,5},{8,10},{9,11},{10,... | collective-permute-start | bytes 1179656 | tf_op jit(solution)/shard_map/ppermute | solution.py:24
  172.1 9.9 %collective-permute-start.46 = (f32[456,384]{1,0:T(8,128)}, f32[456,384]{1,0:T(8,128)}, u32[]{:S(2)}, u32[]{:S(2)}) collective-permute-start(f32[456,384]{1,0:T(8,128)} %get-tuple-element.218), channel_id=1, source_target_pairs={{0,1},{1,0},{2,3},{3,2},{4,5},{5,4},{6,7},{7,6},{8,9},{9,8},{10,11... | collective-permute-start | bytes 2101256 | tf_op jit(solution)/shard_map/ppermute | solution.py:24
  186.5 12.9 %collective-permute-start.49 = (f32[448,384]{1,0:T(8,128)}, f32[448,384]{1,0:T(8,128)}, u32[]{:S(2)}, u32[]{:S(2)}) collective-permute-start(f32[448,384]{1,0:T(8,128)} %get-tuple-element.230), channel_id=1, source_target_pairs={{0,1},{1,0},{2,3},{3,2},{4,5},{5,4},{6,7},{7,6},{8,9},{9,8},{10,11... | collective-permute-start | bytes 2064392 | tf_op jit(solution)/shard_map/ppermute | solution.py:24
  186.5 15.3 %collective-permute-start.48 = (f32[448,384]{1,0:T(8,128)}, f32[448,384]{1,0:T(8,128)}, u32[]{:S(2)}, u32[]{:S(2)}) collective-permute-start(f32[448,384]{1,0:T(8,128)} %get-tuple-element.228), channel_id=1, source_target_pairs={{0,1},{1,0},{2,3},{3,2},{4,5},{5,4},{6,7},{7,6},{8,9},{9,8},{10,11... | collective-permute-start | bytes 2064392 | tf_op jit(solution)/shard_map/ppermute | solution.py:24
  187.1 16.6 %collective-permute-start.47 = (f16[464,384]{1,0:T(8,128)(2,1)}, f16[464,384]{1,0:T(8,128)(2,1)}, u32[]{:S(2)}, u32[]{:S(2)}) collective-permute-start(f16[464,384]{1,0:T(8,128)(2,1)} %concatenate.88), channel_id=1, source_target_pairs={{0,2},{1,3},{2,0},{3,1},{4,6},{5,7},{6,4},{7,5},{8,10},{9,11},{10,... | collective-permute-start | bytes 1069064 | tf_op jit(solution)/shard_map/ppermute | solution.py:24
  205.9 16.0 %collective-permute-start.55 = (f32[448,384]{1,0:T(8,128)}, f32[448,384]{1,0:T(8,128)}, u32[]{:S(2)}, u32[]{:S(2)}) collective-permute-start(f32[448,384]{1,0:T(8,128)} %copy-done.18), channel_id=1, source_target_pairs={{0,1},{1,0},{2,3},{3,2},{4,5},{5,4},{6,7},{7,6},{8,9},{9,8},{10,11... | collective-permute-start | bytes 2064392 | tf_op jit(solution)/shard_map/ppermute | solution.py:24
  206.2 17.4 %collective-permute-start.54 = (f32[448,384]{1,0:T(8,128)}, f32[448,384]{1,0:T(8,128)}, u32[]{:S(2)}, u32[]{:S(2)}) collective-permute-start(f32[448,384]{1,0:T(8,128)} %copy-done.17), channel_id=1, source_target_pairs={{0,1},{1,0},{2,3},{3,2},{4,5},{5,4},{6,7},{7,6},{8,9},{9,8},{10,11... | collective-permute-start | bytes 2064392 | tf_op jit(solution)/shard_map/ppermute | solution.py:24
  208.1 18.6 %collective-permute-start.50 = (f16[464,384]{1,0:T(8,128)(2,1)S(1)}, f16[464,384]{1,0:T(8,128)(2,1)S(1)}, u32[]{:S(2)}, u32[]{:S(2)}) collective-permute-start(f16[464,384]{1,0:T(8,128)(2,1)S(1)} %concatenate.89), channel_id=1, source_target_pairs={{0,8},{1,9},{2,10},{3,11},{4,12},{5,13},{6,14},{7,15},{8,0},{9,1},... | collective-permute-start | bytes 1069064 | tf_op jit(solution)/shard_map/ppermute | solution.py:33
  212.1 12.7 %collective-permute-start.51 = (f16[448,384]{1,0:T(8,128)(2,1)S(1)}, f16[448,384]{1,0:T(8,128)(2,1)S(1)}, u32[]{:S(2)}, u32[]{:S(2)}) collective-permute-start(f16[448,384]{1,0:T(8,128)(2,1)S(1)} %copy-done.24), channel_id=1, source_target_pairs={{0,2},{1,3},{2,0},{3,1},{4,6},{5,7},{6,4},{7,5},{8,10},{9,11},{10,... | collective-permute-start | bytes 1032200 | tf_op jit(solution)/shard_map/ppermute | solution.py:24
  213.7 14.9 %collective-permute-start.53 = (f16[448,384]{1,0:T(8,128)(2,1)S(1)}, f16[448,384]{1,0:T(8,128)(2,1)S(1)}, u32[]{:S(2)}, u32[]{:S(2)}) collective-permute-start(f16[448,384]{1,0:T(8,128)(2,1)S(1)} %multiply_convert_fusion.4), channel_id=1, source_target_pairs={{0,2},{1,3},{2,0},{3,1},{4,6},{5,7},{6,4},{7,5},{8,10},{9,11},{10,... | collective-permute-start | bytes 1032200 | tf_op jit(solution)/shard_map/ppermute | solution.py:24
  232.9 9.2 %collective-permute-start.60 = (f16[448,384]{1,0:T(8,128)(2,1)S(1)}, f16[448,384]{1,0:T(8,128)(2,1)S(1)}, u32[]{:S(2)}, u32[]{:S(2)}) collective-permute-start(f16[448,384]{1,0:T(8,128)(2,1)S(1)} %multiply_convert_fusion.3), channel_id=1, source_target_pairs={{0,2},{1,3},{2,0},{3,1},{4,6},{5,7},{6,4},{7,5},{8,10},{9,11},{10,... | collective-permute-start | bytes 1032200 | tf_op jit(solution)/shard_map/ppermute | solution.py:24
  235.1 9.5 %collective-permute-start.58 = (f16[464,384]{1,0:T(8,128)(2,1)S(1)}, f16[464,384]{1,0:T(8,128)(2,1)S(1)}, u32[]{:S(2)}, u32[]{:S(2)}) collective-permute-start(f16[464,384]{1,0:T(8,128)(2,1)S(1)} %concatenate.91), channel_id=1, source_target_pairs={{0,12},{1,13},{2,14},{3,15},{4,0},{5,1},{6,2},{7,3},{8,4},{9,5},{1... | collective-permute-start | bytes 1069064 | tf_op jit(solution)/shard_map/ppermute | solution.py:33
  235.4 16.8 %collective-permute-start.56 = (f16[464,384]{1,0:T(8,128)(2,1)S(1)}, f16[464,384]{1,0:T(8,128)(2,1)}, u32[]{:S(2)}, u32[]{:S(2)}) collective-permute-start(f16[464,384]{1,0:T(8,128)(2,1)S(1)} %concatenate.90), channel_id=1, source_target_pairs={{0,4},{1,5},{2,6},{3,7},{4,8},{5,9},{6,10},{7,11},{8,12},{9,13},{1... | collective-permute-start | bytes 1069064 | tf_op jit(solution)/shard_map/ppermute | solution.py:33
  (65 other events, 241.6 us)
